TPU v7x, 1024 devices: a whole 4x8x16 slice. The times are simulated.
1024 devices in a mesh: node: 128 (over z, x, core), local: 8 (over y).
Axes of the slice: x: 4, y: 8, z: 16, core: 2. Of those that a mesh axis runs over, the one named last changes fastest.
Arguments:
- grad_out: bfloat16 [4096, 3584], P('node', 'local'), may hold values from -6 to 6
- expert_ids: int32 [4096, 8], replicated, may hold values from 0 to 255, as said below
- row_slots: int32 [4096, 8], replicated, may hold values from 0 to 127, as said below
- combine: float32 [4096, 8], replicated, may hold values from 0.2 to 1.5
- down_weight: bfloat16 [256, 1024, 3584], P('node', None, 'local'), may hold values from -0.09375 to 0.09375
- gate_pre: bfloat16 [256, 128, 1024], P('node', None, 'local'), may hold values from -6 to 6
- up_pre: bfloat16 [256, 128, 1024], P('node', None, 'local'), may hold values from -3 to 3
Outputs:
- d_gate: bfloat16 [256, 128, 1024], P('node', None, 'local')
- d_up: bfloat16 [256, 128, 1024], P('node', None, 'local')
- d_combine: float32 [4096, 8], P('node')
Inputs may be any that keep to these rules, and one draw needn't show every extreme that they name: `expert_ids`: each token names 8 different experts, two on each of 4 nodes (expert e lies on node e // 2). The tokens of one index of node choose any one node in at most 1 token, and some pair of nodes reaches 1. `row_slots`: every pair of an expert and a row is named by exactly one choice of one token.
All inputs are finite; a program needn't handle non-finite values.
Results may differ from a plain program's by a relative error of at most 0.0015.
Values may be sent and summed in bfloat16 or wider, within the bound.
A program may use at most 32 MiB of HBM per device.

v0:
```python
import jax
import jax.numpy as jnp
from jax import lax
from jax.sharding import PartitionSpec as P


def shards(grad_out, expert_ids, row_slots, combine, down_weight, gate_pre, up_pre):
    exp_here = down_weight.shape[0]
    cap = gate_pre.shape[1]
    tok_here = grad_out.shape[0]
    width_here = grad_out.shape[1]
    flat = expert_ids * cap + row_slots
    owner = jnp.repeat(jnp.arange(flat.shape[0], dtype=jnp.int32), flat.shape[1])
    node_at = lax.axis_index("node")
    first_row = node_at * (exp_here * cap)
    wanted = first_row + jnp.arange(exp_here * cap, dtype=jnp.int32)
    blocks = 4
    flat_blocks = flat.reshape(blocks, -1)
    owner_blocks = owner.reshape(blocks, -1)
    weight_blocks = combine.reshape(blocks, -1)

    def match_block(carry, block):
        entry_rows, entry_owner, entry_weight = block
        match = entry_rows[:, None] == wanted[None, :]
        found_token = jnp.sum(jnp.where(match, entry_owner[:, None], 0), axis=0)
        found_weight = jnp.sum(jnp.where(match, entry_weight[:, None], 0.0), axis=0)
        return ((carry[0] + found_token, carry[1] + found_weight), None)

    start_carry = (
        jnp.zeros((exp_here * cap,), jnp.int32),
        jnp.zeros((exp_here * cap,), jnp.float32),
    )
    (here_token, weight_flat), unused = lax.scan(
        match_block, start_carry, (flat_blocks, owner_blocks, weight_blocks)
    )
    here_weight = weight_flat.reshape(exp_here, cap)
    gathered = lax.all_gather(grad_out, "node", axis=0, tiled=True)
    picked = gathered[here_token]
    rows = picked.reshape(exp_here, cap, width_here)
    partial_proj = jnp.einsum("ecd,ehd->ech", rows, down_weight, preferred_element_type=jnp.float32)
    projected = lax.psum_scatter(partial_proj, "local", scatter_dimension=2, tiled=True)
    gate_wide = gate_pre.astype(jnp.float32)
    up_wide = up_pre.astype(jnp.float32)
    logistic = jax.nn.sigmoid(gate_wide)
    activated = gate_wide * logistic
    hidden = activated * up_wide
    grad_hidden = here_weight[:, :, None] * projected
    d_gate = (grad_hidden * up_wide * logistic * (1.0 + gate_wide * (1.0 - logistic))).astype(
        jnp.bfloat16
    )
    d_up = (grad_hidden * activated).astype(jnp.bfloat16)
    score_part = jnp.sum(hidden * projected, axis=2)
    score_total = lax.psum(score_part, "local")
    table = lax.all_gather(score_total, "node", axis=0, tiled=True).reshape(-1)
    own_flat = lax.dynamic_slice_in_dim(flat, node_at * tok_here, tok_here)
    d_combine = table[own_flat]
    return (d_gate, d_up, d_combine)


def solution(mesh):
    return jax.shard_map(
        shards,
        mesh=mesh,
        in_specs=(
            P("node", "local"),
            P(),
            P(),
            P(),
            P("node", None, "local"),
            P("node", None, "local"),
            P("node", None, "local"),
        ),
        out_specs=(P("node", None, "local"), P("node", None, "local"), P("node", None)),
        check_vma=False,
    )
```

profile of v0, /device:TPU:1, one launch (start us, length us, event | category | flops | bytes accessed | tf_op | source)
XLA Modules:
  0.0 329.5 jit_solution(15352986126645946455)
XLA Ops:
  8.0 1.0 multiply_add_fusion
  9.0 1.9 copy.23
  10.9 2.7 reshape.26
  13.6 1.9 copy.24
  15.6 2.7 reshape.27
  18.3 1.5 broadcast_in_dim.45
  19.7 2.7 reshape_reshape.3
  22.5 23.0 %while.13 = (s32[]{:T(128)}, s32[256]{0:T(256)S(1)}, f32[256]{0:T(256)S(1)}, s32[4,8192]{1,0:T(4,128)S(1)}, s32[4,8192]{1,0:T(4,128)S(1)}, /*index=5*/f32[4,8192]{1,0:T(4,128)S(1)}, s32[]{:T(128)}, s32[]{:T(128)}, s32[]{:T(128)}) while((s32[]{:T(128)}, s32[256]{0:T(256)S(1)}, f32[256]{0:T(256)S(1)}, s32[4,8192]{1,0:T(4,128)S(1)}, ...), condition=%wide.region_3.4_spmd.clone, body=%wide.region_0.3_spmd.clone.sunk | while | flops 12583683 | bytes 339060 | solution.py:33
  22.6 2.8 fusion.18
  25.4 2.8 fusion.19
  28.3 2.8 fusion.18
  31.2 2.8 fusion.19
  34.1 2.8 fusion.18
  36.9 2.8 fusion.19
  39.8 2.8 fusion.18
  42.7 2.8 fusion.19
  45.5 125.0 %all-gather.3.cloned.1.call-done = bf16[4096,448]{1,0:T(8,128)(2,1)} async-done(((bf16[32,448]{1,0:T(8,128)(2,1)}), bf16[4096,448]{1,0:T(8,128)(2,1)}) %all-gather.3.cloned.1.call-update) | async-done | bytes 3670032 | tf_op jit(solution)/shard_map/all_gather | solution.py:37
  170.5 3.9 %gather_fusion = bf16[256,448]{1,0:T(8,128)(2,1)S(1)} fusion(bf16[4096,448]{1,0:T(8,128)(2,1)} %all-gather.3.cloned.1.call-done, s32[1024]{0:T(1024)S(1)} %pad_clamp_fusion.1), kind=kCustom, calls=%fused_computation | custom fusion | bytes 459776 | tf_op jit(solution)/shard_map/gather | solution.py:38
  174.5 1.4 fusion.13
  176.2 36.2 %reduce-scatter.2.cloned.1.call-done = f32[2,128,128]{2,1,0:T(8,128)} async-done(((f32[2,128,1024]{2,1,0:T(8,128)}), f32[2,128,128]{2,1,0:T(8,128)}) %reduce-scatter.2.cloned.1.call-update) | async-done | bytes 131088 | tf_op jit(solution)/shard_map/reduce_scatter | solution.py:41
  212.4 1.7 fusion.8
  214.1 11.8 %psum.7 = f32[2,128]{1,0:T(2,128)S(1)} all-reduce(f32[2,128]{1,0:T(2,128)S(1)} %get-tuple-element.95), channel_id=1, replica_groups=mesh['node'=128,'local'=8] {'local'}, use_global_device_ids=true, to_apply=%region_6.7 | all-reduce | flops 256 | bytes 2048 | tf_op jit(solution)/shard_map/psum | solution.py:53
  225.9 94.3 %all-gather = f32[128,2,128]{2,1,0:T(2,128)S(1)} all-gather(f32[1,2,128]{2,1,0:T(2,128)S(1)} %bitcast.22), channel_id=1, replica_groups=mesh['node'=128,'local'=8] {'node'}, dimensions={0}, use_global_device_ids=true | all-gather | bytes 132096 | tf_op jit(solution)/shard_map/all_gather | solution.py:54
  320.2 1.7 gather_fusion.1
  (42 shorter events, 2.4 us)
Async XLA Ops:
  7.2 167.3 %copy-start = (bf16[2,1024,448]{1,2,0:T(8,128)(2,1)S(1)}, bf16[2,1024,448]{1,2,0:T(8,128)(2,1)}, u32[]{:S(2)}) copy-start(bf16[2,1024,448]{1,2,0:T(8,128)(2,1)} %param.13) | copy-start | bytes 5505028
  7.2 6.4 %copy-start.1 = (f32[4096,8]{0,1:T(8,128)S(1)}, f32[4096,8]{0,1:T(8,128)}, u32[]{:S(2)}) copy-start(f32[4096,8]{0,1:T(8,128)} %param.12) | copy-start | bytes 393220
  7.2 163.3 %all-gather.3.cloned.1.call-start = ((), (), s32[]{:S(2)}) async-start(), calls=%async_computation.1 | async-start | bytes 4227072 | tf_op jit(solution)/shard_map/all_gather | solution.py:37
  7.9 204.4 %reduce-scatter.2.cloned.1.call-start = ((), (), s32[]{:S(2)}) async-start(), calls=%async_computation.2 | async-start | bytes 1179648 | tf_op jit(solution)/shard_map/reduce_scatter | solution.py:41
  22.4 189.9 %copy-start.2 = (bf16[2,128,128]{2,1,0:T(8,128)(2,1)S(1)}, bf16[2,128,128]{2,1,0:T(8,128)(2,1)}, u32[]{:S(2)}) copy-start(bf16[2,128,128]{2,1,0:T(8,128)(2,1)} %param.15) | copy-start | bytes 196612
  22.5 189.9 %copy-start.3 = (bf16[2,128,128]{2,1,0:T(8,128)(2,1)S(1)}, bf16[2,128,128]{2,1,0:T(8,128)(2,1)}, u32[]{:S(2)}) copy-start(bf16[2,128,128]{2,1,0:T(8,128)(2,1)} %param.14) | copy-start | bytes 196612
Sparse Core Ops, SparseCore 0:
  12.3 158.1 all-gather.2
  176.0 36.2 reduce-scatter.1
where the time goes:
time: 330 us; the launch traced here: 329 us
  waiting for transfers between devices  162 us (49%)
  blocking collectives  106 us (32%)
  other arithmetic  25.2 us (8%)
  local copies, waits for them, and re-layouts  20.5 us (6%)
  between operations  14.2 us (4%)
    all_gather x1, waiting for transfers between devices, shards(): gathered = lax.all_gather(grad_out, 'node', axis=0, tiled=True)  125 us
    all_gather x1, blocking collectives, shards(): table = lax.all_gather(score_total, 'node', axis=0, tiled=True).reshape(-1)  94.3 us
    reduce_scatter x1, waiting for transfers between devices, shards(): lax.psum_scatter(partial_proj, 'local', scatter_dimension=2, tiled=True)  36.2 us
    psum x1, blocking collectives, shards(): score_total = lax.psum(score_part, 'local')  11.8 us
    reduce_sum x4, other arithmetic, match_block(): found_weight = jnp.sum(jnp.where(match, entry_weight[:, None], 0.0), axis=0)  11.1 us
    reduce_sum x4, other arithmetic, match_block(): found_token = jnp.sum(jnp.where(match, entry_owner[:, None], 0), axis=0)  11.1 us
  transfers between devices with their start and end apart: 2, of which 2 were waited for; matrix products, arithmetic and copies ran while one was open for 11% of the time, Pallas kernels for 0%

commit v1 on v0

v1 whole, which is shorter than its diff:
```python
import jax
import jax.numpy as jnp
from jax import lax
from jax.experimental import pallas as pl
from jax.experimental.pallas import tpu as pltpu
from jax.sharding import PartitionSpec as P

MESH = pl.DeviceIdType.MESH
NP = 8
NZ = 16
NN = NP * NZ
NL = 8
CAP = 128
HB = 128
DL = 448
DPAD = 512
F32 = jnp.float32
BF16 = jnp.bfloat16
EXACT = lax.Precision.HIGHEST


def dot(a, b):
    return jnp.dot(a, b, preferred_element_type=F32)


def one_hot(cond, dtype=BF16):
    return jnp.where(cond, 1.0, 0.0).astype(dtype)


def iota(shape, dim):
    return lax.broadcasted_iota(jnp.int32, shape, dim)


def turn(i):
    half = lax.div(i + 1, 2)
    return 4 + half * (1 - 2 * lax.rem(i, 2))


def kernel(
    ids_ref, slots_ref, comb_ref, g_ref, w_hbm, gate_ref, up_ref,
    dg_ref, du_ref, dc_ref,
    s1, r1, s2, r2, wv, xs, gm, gsel, a_gate, a_up, hid, qs, qr, cs, cr, acc,
    ys, yr, ps, pr, zs, zr,
    w_sem, s1_sem, r1_sem, s2_sem, r2_sem, qs_sem, qr_sem, cs_sem, cr_sem,
    ys_sem, yr_sem, ps_sem, pr_sem, zs_sem, zr_sem,
):
    node = lax.axis_index("node")
    loc = lax.axis_index("local")
    zi = lax.div(node, NP)
    pi = lax.rem(node, NP)

    w_copy = pltpu.make_async_copy(w_hbm, wv, w_sem)
    w_copy.start()

    def p_peer(d):
        return lax.rem(pi + d, NP)

    def z_peer(d):
        return lax.rem(zi + d, NZ)

    def l_peer(d):
        return lax.rem(loc + d, NL)

    barrier = pltpu.get_barrier_semaphore()

    def greet_p(d, c):
        pl.semaphore_signal(barrier, inc=1, device_id=(zi * NP + p_peer(d), loc), device_id_type=MESH)
        pl.semaphore_signal(barrier, inc=1, device_id=(node, l_peer(d)), device_id_type=MESH)
        return c

    def greet_z(d, c):
        pl.semaphore_signal(barrier, inc=1, device_id=(z_peer(d) * NP + pi, loc), device_id_type=MESH)
        return c

    lax.fori_loop(1, NP, greet_p, 0)
    lax.fori_loop(1, NZ, greet_z, 0)

    base = pl.multiple_of(lax.div(node, 4) * 128, 128)
    ids_c = ids_ref[:, pl.ds(base, 128)]
    sub = lax.rem(node, 4)
    ids_my = ids_c[:, 0:32]
    for j in range(1, 4):
        ids_my = jnp.where(sub == j, ids_c[:, 32 * j : 32 * j + 32], ids_my)
    dest = ids_my >> 1
    i = iota((NN, 32), 0)
    dest_of = (i & (NZ - 1)) * NP + (i >> 4)
    hit = jnp.zeros((NN, 32), F32)
    for k in range(8):
        hit = jnp.where(dest_of == dest[k : k + 1, :], 1.0, hit)
    x = dot(hit.astype(BF16), g_ref[...]).astype(BF16)
    s1[:, :, 0:DL] = x.reshape(NP, NZ, DL)
    s1[:, :, DL:DPAD] = jnp.zeros((NP, NZ, DPAD - DL), BF16)

    pl.semaphore_wait(barrier, 2 * (NP - 1) + NZ - 1)

    def s1_copy(d, src, dst):
        return pltpu.make_async_remote_copy(
            src_ref=s1.at[src], dst_ref=r1.at[dst],
            send_sem=s1_sem.at[d], recv_sem=r1_sem.at[d],
            device_id=(zi * NP + p_peer(d), loc), device_id_type=MESH,
        )

    def s1_start(d, c):
        s1_copy(d, p_peer(d), pi).start()
        return c

    lax.fori_loop(1, NP, s1_start, 0)
    r1[pl.ds(pi, 1)] = s1[pl.ds(pi, 1)]

    ri = iota((2 * NN, NN), 0)
    ci = iota((2 * NN, NN), 1)
    want = (ri & (NP - 1)) * NZ + (ri >> 4)
    half = (ri >> 3) & 1
    perm0 = one_hot((ci == want) & (half == 0))
    perm1 = one_hot((ci == want) & (half == 1))

    def s1_wait(d, c):
        s1_copy(d, p_peer(d), lax.rem(pi + NP - d, NP)).wait_recv()
        return c

    lax.fori_loop(1, NP, s1_wait, 0)
    r1f = r1[...].reshape(NN, DPAD)
    s2v = dot(perm0, r1f[:, 0:256]) + dot(perm1, r1f[:, 256:512])
    s2[...] = s2v.astype(BF16).reshape(NZ, 16, 256)

    def s2_copy(d, src, dst):
        return pltpu.make_async_remote_copy(
            src_ref=s2.at[src], dst_ref=r2.at[dst],
            send_sem=s2_sem.at[d], recv_sem=r2_sem.at[d],
            device_id=(z_peer(d) * NP + pi, loc), device_id_type=MESH,
        )

    def s2_start(d, c):
        s2_copy(d, z_peer(d), zi).start()
        return c

    lax.fori_loop(1, NZ, s2_start, 0)
    r2[pl.ds(zi, 1)] = s2[pl.ds(zi, 1)]

    ids = ids_ref[...]
    slots = slots_ref[...].astype(F32)
    comb = comb_ref[...]
    spread = (iota((128, NN), 0) >> 5) == (iota((128, NN), 1) & 3)
    spread_b = one_hot(spread)
    spread_f = one_hot(spread, F32)
    rows_here = (iota((256, NN), 0) >> 3) == (iota((256, NN), 1) >> 2)

    def stack(v):
        return jnp.concatenate([v[:, c * 128 : (c + 1) * 128] for c in range(32)], axis=0)

    nn = iota((NN, 256), 0)
    cc = iota((NN, 256), 1)
    place = (nn >> 3) * 16 + (nn & 7)
    ex0 = one_hot(cc == place)
    ex1 = one_hot(cc == place + 8)
    si = iota((CAP, NN), 0).astype(F32)
    for e in range(2):
        mine = ids == 2 * node + e
        slot_y = dot(stack(jnp.where(mine, slots, 0.0)).astype(BF16), spread_b)
        slot_n = jnp.sum(jnp.where(rows_here, slot_y, 0.0), axis=0, keepdims=True)
        comb_y = jnp.dot(
            stack(jnp.where(mine, comb, 0.0)), spread_f, precision=EXACT, preferred_element_type=F32
        )
        comb_n = jnp.sum(jnp.where(rows_here, comb_y, 0.0), axis=0, keepdims=True)
        sel = si == slot_n
        sel_f = jnp.where(sel, 1.0, 0.0)
        gm[e] = sel_f
        weight = jnp.sum(jnp.where(sel, comb_n, 0.0), axis=1, keepdims=True)
        sel_b = sel_f.astype(BF16)
        gsel[e, 0] = dot(sel_b, ex0).astype(BF16)
        gsel[e, 1] = dot(sel_b, ex1).astype(BF16)
        g = gate_ref[e].astype(F32)
        u = up_ref[e].astype(F32)
        sg = 1.0 / (1.0 + jnp.exp(-g))
        gs = g * sg
        hid[e] = gs * u
        a_up[e] = weight * gs
        a_gate[e] = weight * (u * sg * (1.0 + g * (1.0 - sg)))

    w_copy.wait()

    def s2_wait(d, c):
        s2_copy(d, z_peer(d), lax.rem(zi + NZ - d, NZ)).wait_recv()
        return c

    lax.fori_loop(1, NZ, s2_wait, 0)
    r2f = r2[...].reshape(256, 256)
    for e in range(2):
        xs[e, :, 0:256] = dot(gsel[e, 0], r2f).astype(BF16)
        xs[e, :, 256:512] = dot(gsel[e, 1], r2f).astype(BF16)

    def q_copy(d, src, dst):
        return pltpu.make_async_remote_copy(
            src_ref=qs.at[src], dst_ref=qr.at[dst],
            send_sem=qs_sem.at[d], recv_sem=qr_sem.at[d],
            device_id=(node, l_peer(d)), device_id_type=MESH,
        )

    def c_copy(d, src, dst):
        return pltpu.make_async_remote_copy(
            src_ref=cs.at[src], dst_ref=cr.at[dst],
            send_sem=cs_sem.at[d], recv_sem=cr_sem.at[d],
            device_id=(node, l_peer(d)), device_id_type=MESH,
        )

    def project(e, l):
        cols = pl.ds(pl.multiple_of(l * HB, HB), HB)
        return dot(xs[e, :, 0:DL], wv[e, :, cols])

    def send_block(i, c):
        d = turn(i)
        l = l_peer(d)
        for e in range(2):
            t = project(e, l)
            top = jnp.maximum(jnp.max(jnp.abs(t), axis=0, keepdims=True), 1e-30)
            q = jnp.round(t * (32767.0 / top))
            qs[l, e] = q.astype(jnp.int32).astype(jnp.int16)
            cs[l, e : e + 1, :] = top * (1.0 / 32767.0)
        c_copy(d, l, loc).start()
        q_copy(d, l, loc).start()
        return c

    lax.fori_loop(0, NL - 1, send_block, 0)
    for e in range(2):
        acc[e] = project(e, loc)

    def take_block(i, c):
        d = turn(i)
        l = lax.rem(loc + NL - d, NL)
        c_copy(d, l_peer(d), l).wait_recv()
        q_copy(d, l_peer(d), l).wait_recv()
        for e in range(2):
            acc[e] += qr[l, e].astype(jnp.int32).astype(F32) * cr[l, e : e + 1, :]
        return c

    lax.fori_loop(0, NL - 1, take_block, 0)

    for e in range(2):
        t = acc[e]
        part = jnp.sum(hid[e] * t, axis=1, keepdims=True)
        ys[e : e + 1, :] = jnp.sum(gm[e] * part, axis=0, keepdims=True)

    def y_copy(d, dst):
        return pltpu.make_async_remote_copy(
            src_ref=ys, dst_ref=yr.at[dst],
            send_sem=ys_sem.at[d], recv_sem=yr_sem.at[d],
            device_id=(node, l_peer(d)), device_id_type=MESH,
        )

    def y_start(d, c):
        y_copy(d, loc).start()
        return c

    lax.fori_loop(1, NL, y_start, 0)
    yr[pl.ds(loc, 1)] = ys[...].reshape(1, 2, NN)
    for e in range(2):
        t = acc[e]
        dg_ref[e] = (t * a_gate[e]).astype(BF16)
        du_ref[e] = (t * a_up[e]).astype(BF16)

    def y_wait(d, c):
        y_copy(d, lax.rem(loc + NL - d, NL)).wait_recv()
        return c

    lax.fori_loop(1, NL, y_wait, 0)
    ps[...] = jnp.sum(yr[...], axis=0)

    def p_copy(d, dst):
        return pltpu.make_async_remote_copy(
            src_ref=ps, dst_ref=pr.at[dst],
            send_sem=ps_sem.at[d], recv_sem=pr_sem.at[d],
            device_id=(zi * NP + p_peer(d), loc), device_id_type=MESH,
        )

    def p_start(d, c):
        p_copy(d, pi).start()
        return c

    lax.fori_loop(1, NP, p_start, 0)
    pr[pl.ds(pi, 1)] = ps[...].reshape(1, 2, NN)

    def p_wait(d, c):
        p_copy(d, lax.rem(pi + NP - d, NP)).wait_recv()
        return c

    lax.fori_loop(1, NP, p_wait, 0)
    to_here = (iota((2, NN), 1) & (NP - 1)) == pi
    packed = jnp.zeros((2, NN), F32)
    for q in range(NP):
        v = jnp.where(to_here, pr[q], 0.0)
        if q:
            v = jnp.concatenate([v[:, NN - q :], v[:, : NN - q]], axis=1)
        packed = packed + v
    zs[...] = packed

    def z_copy(d, dst):
        return pltpu.make_async_remote_copy(
            src_ref=zs, dst_ref=zr.at[dst],
            send_sem=zs_sem.at[d], recv_sem=zr_sem.at[d],
            device_id=(z_peer(d) * NP + pi, loc), device_id_type=MESH,
        )

    def z_start(d, c):
        z_copy(d, zi).start()
        return c

    lax.fori_loop(1, NZ, z_start, 0)
    zr[pl.ds(zi, 1)] = packed.reshape(1, 2, NN)

    choice = jnp.concatenate([ids_my[k : k + 1, :] for k in range(8)], axis=1)
    lane = (node + ((choice >> 1) & (NP - 1))) & (NN - 1)
    lane_hit = iota((NN, 256), 0) == lane
    plane_hit = iota((NZ, 256), 0) == (choice >> 4)
    member = choice & 1

    def z_wait(d, c):
        z_copy(d, lax.rem(zi + NZ - d, NZ)).wait_recv()
        return c

    lax.fori_loop(1, NZ, z_wait, 0)
    found = jnp.zeros((NN, 256), F32)
    for m in range(2):
        pick = jnp.where(plane_hit & (member == m), 1.0, 0.0)
        found = found + lax.dot_general(
            zr[:, m, :], pick, (((0,), (0,)), ((), ())), precision=EXACT, preferred_element_type=F32
        )
    flat = jnp.sum(jnp.where(lane_hit, found, 0.0), axis=0, keepdims=True)
    for k in range(8):
        dc_ref[k : k + 1, :] = flat[:, 32 * k : 32 * k + 32]

    def drain8(d, c):
        s1_copy(d, p_peer(d), pi).wait_send()
        q_copy(d, l_peer(d), loc).wait_send()
        c_copy(d, l_peer(d), loc).wait_send()
        y_copy(d, loc).wait_send()
        p_copy(d, pi).wait_send()
        return c

    def drain16(d, c):
        s2_copy(d, z_peer(d), zi).wait_send()
        z_copy(d, zi).wait_send()
        return c

    lax.fori_loop(1, NP, drain8, 0)
    lax.fori_loop(1, NZ, drain16, 0)


def shards(grad_out, expert_ids, row_slots, combine, down_weight, gate_pre, up_pre):
    vmem = pl.BlockSpec(memory_space=pltpu.VMEM)
    dma = pltpu.SemaphoreType.DMA
    d_gate, d_up, d_combine = pl.pallas_call(
        kernel,
        out_shape=(
            jax.ShapeDtypeStruct(gate_pre.shape, BF16),
            jax.ShapeDtypeStruct(gate_pre.shape, BF16),
            jax.ShapeDtypeStruct((8, 32), F32),
        ),
        in_specs=[vmem, vmem, vmem, vmem, pl.BlockSpec(memory_space=pl.ANY), vmem, vmem],
        out_specs=(vmem, vmem, vmem),
        scratch_shapes=[
            pltpu.VMEM((NP, NZ, DPAD), BF16),
            pltpu.VMEM((NP, NZ, DPAD), BF16),
            pltpu.VMEM((NZ, 16, 256), BF16),
            pltpu.VMEM((NZ, 16, 256), BF16),
            pltpu.VMEM((2, DL, 1024), BF16),
            pltpu.VMEM((2, CAP, DPAD), BF16),
            pltpu.VMEM((2, CAP, NN), F32),
            pltpu.VMEM((2, 2, CAP, 256), BF16),
            pltpu.VMEM((2, CAP, HB), F32),
            pltpu.VMEM((2, CAP, HB), F32),
            pltpu.VMEM((2, CAP, HB), F32),
            pltpu.VMEM((NL, 2, CAP, HB), jnp.int16),
            pltpu.VMEM((NL, 2, CAP, HB), jnp.int16),
            pltpu.VMEM((NL, 2, HB), F32),
            pltpu.VMEM((NL, 2, HB), F32),
            pltpu.VMEM((2, CAP, HB), F32),
            pltpu.VMEM((2, NN), F32),
            pltpu.VMEM((NL, 2, NN), F32),
            pltpu.VMEM((2, NN), F32),
            pltpu.VMEM((NP, 2, NN), F32),
            pltpu.VMEM((2, NN), F32),
            pltpu.VMEM((NZ, 2, NN), F32),
            dma,
            dma((NP,)), dma((NP,)),
            dma((NZ,)), dma((NZ,)),
            dma((NL,)), dma((NL,)),
            dma((NL,)), dma((NL,)),
            dma((NL,)), dma((NL,)),
            dma((NP,)), dma((NP,)),
            dma((NZ,)), dma((NZ,)),
        ],
        compiler_params=pltpu.CompilerParams(
            collective_id=0, has_side_effects=True, vmem_limit_bytes=32 * 1024 * 1024
        ),
        name="routed_backward",
    )(
        expert_ids.T, row_slots.T, combine.T, grad_out,
        jnp.swapaxes(down_weight, 1, 2), gate_pre, up_pre,
    )
    return d_gate, d_up, d_combine.T


def solution(mesh):
    return jax.shard_map(
        shards,
        mesh=mesh,
        in_specs=(
            P("node", "local"),
            P(),
            P(),
            P(),
            P("node", None, "local"),
            P("node", None, "local"),
            P("node", None, "local"),
        ),
        out_specs=(P("node", None, "local"), P("node", None, "local"), P("node", None)),
        check_vma=False,
    )
```

time: 330 us -> 78.6 us (0.24)
  waiting for transfers between devices: 162 us -> 0 us
  blocking collectives: 106 us -> 0 us
  Pallas kernels: 0 us -> 69 us
  other arithmetic: 25.2 us -> 0 us
  between operations: 14.2 us -> 0.66 us
  local copies, waits for them, and re-layouts: 20.5 us -> 8.49 us
    all_gather x1 -> x0, waiting for transfers between devices: 125 us -> none  [shards(): gathered = lax.all_gather(grad_out, 'node', axis=0, tiled=True)]
    all_gather x1 -> x0, blocking collectives: 94.3 us -> none  [shards(): table = lax.all_gather(score_total, 'node', axis=0, tiled=True).reshape(-1)]
    pallas_call x0 -> x1, Pallas kernels: none -> 69 us  [shards(): pl.pallas_call(kernel, out_shape=(jax.ShapeDtypeStruct(gate_pre.shape, BF...]
    reduce_scatter x1 -> x0, waiting for transfers between devices: 36.2 us -> none  [shards(): lax.psum_scatter(partial_proj, 'local', scatter_dimension=2, tiled=True)]
    reduce_sum x9 -> x0, other arithmetic: 24 us -> none  [the longest x4 11.1 us: match_block(): found_weight = jnp.sum(jnp.where(match, entry_weight[:, None], 0.0), axis=0)]
    psum x1 -> x0, blocking collectives: 11.8 us -> none  [shards(): score_total = lax.psum(score_part, 'local')]
    unnamed x10 -> x17, local copies, waits for them, and re-layouts: 2.64 us -> 8.49 us
    gather x3 -> x0, local copies, waits for them, and re-layouts: 5.74 us -> none  [the longest x1 3.94 us: shards(): picked = gathered[here_token]]
  transfers between devices with their start and end apart: 2 -> 0, of which waited for: 2 -> 0; matrix products, arithmetic and copies ran while one was open for 11% -> 0% of each run, Pallas kernels for 0% -> 0%
where the time goes in v1:
time: 78.6 us; the launch traced here: 78.2 us
  Pallas kernels  69 us (88%)
  local copies, waits for them, and re-layouts  8.49 us (11%)
    pallas_call x1, Pallas kernels, shards(): pl.pallas_call(kernel, out_shape=(jax.ShapeDtypeStruct(gate_pre.shape, BF...  69 us
    unnamed x17, local copies, waits for them, and re-layouts  8.49 us

profile of v1, /device:TPU:1, one launch (start us, length us, event | category | flops | bytes accessed | tf_op | source)
XLA Modules:
  0.0 78.2 jit_solution(11510859269092944196)
XLA Ops:
  0.6 0.0 copy-start
  0.6 1.5 %copy-done = bf16[2,1024,448]{1,2,0:T(8,128)(2,1)S(1)} copy-done((bf16[2,1024,448]{1,2,0:T(8,128)(2,1)S(1)}, bf16[2,1024,448]{1,2,0:T(8,128)(2,1)}, u32[]{:S(2)}) %copy-start) | copy-done | bytes 1835032
  2.1 0.0 copy-start.1
  2.1 0.9 %copy-done.1 = s32[4096,8]{0,1:T(8,128)S(1)} copy-done((s32[4096,8]{0,1:T(8,128)S(1)}, s32[4096,8]{0,1:T(8,128)}, u32[]{:S(2)}) %copy-start.1) | copy-done | bytes 131096
  3.0 0.0 copy-start.2
  3.0 0.9 %copy-done.2 = s32[4096,8]{0,1:T(8,128)S(1)} copy-done((s32[4096,8]{0,1:T(8,128)S(1)}, s32[4096,8]{0,1:T(8,128)}, u32[]{:S(2)}) %copy-start.2) | copy-done | bytes 131096
  3.9 0.0 copy-start.3
  3.9 0.9 %copy-done.3 = f32[4096,8]{0,1:T(8,128)S(1)} copy-done((f32[4096,8]{0,1:T(8,128)S(1)}, f32[4096,8]{0,1:T(8,128)}, u32[]{:S(2)}) %copy-start.3) | copy-done | bytes 131096
  4.8 0.0 copy-start.4
  4.8 0.8 %copy-done.4 = bf16[2,128,128]{2,1,0:T(8,128)(2,1)S(1)} copy-done((bf16[2,128,128]{2,1,0:T(8,128)(2,1)S(1)}, bf16[2,128,128]{2,1,0:T(8,128)(2,1)}, u32[]{:S(2)}) %copy-start.4) | copy-done | bytes 65560
  5.7 0.0 copy-start.5
  5.7 0.8 %copy-done.5 = bf16[2,128,128]{2,1,0:T(8,128)(2,1)S(1)} copy-done((bf16[2,128,128]{2,1,0:T(8,128)(2,1)S(1)}, bf16[2,128,128]{2,1,0:T(8,128)(2,1)}, u32[]{:S(2)}) %copy-start.5) | copy-done | bytes 65560
  6.5 0.0 copy-start.6
  6.5 0.8 copy-done.6
  7.3 69.0 %routed_backward.1 = (bf16[2,128,128]{2,1,0:T(8,128)(2,1)S(1)}, bf16[2,128,128]{2,1,0:T(8,128)(2,1)S(1)}, f32[8,32]{1,0:T(8,128)S(1)}) custom-call(s32[8,4096]{1,0:T(8,128)S(1)} %bitcast.6, s32[8,4096]{1,0:T(8,128)S(1)} %bitcast.7, f32[8,4096]{1,0:T(8,128)S(1)} %bitcast.8, bf16[32,448]{1,0:T(8,128)(2,1)S(1)} %copy-done.6, bf16[2,448,1024]{2,1,0:T(8,128)(2,1)S(1)} %bitcast.5, ...), custom_call_target="tpu_custom_call" | custom-call | tf_op jit(solution)/shard_map/routed_backward/pallas_call | solution.py:351
  76.3 0.6 copy.13
  77.0 0.6 copy.14
  77.6 0.6 copy.15
Async XLA Ops:
  0.6 1.5 %copy-start = (bf16[2,1024,448]{1,2,0:T(8,128)(2,1)S(1)}, bf16[2,1024,448]{1,2,0:T(8,128)(2,1)}, u32[]{:S(2)}) copy-start(bf16[2,1024,448]{1,2,0:T(8,128)(2,1)} %param.11) | copy-start | bytes 5505028
  2.1 0.9 %copy-start.1 = (s32[4096,8]{0,1:T(8,128)S(1)}, s32[4096,8]{0,1:T(8,128)}, u32[]{:S(2)}) copy-start(s32[4096,8]{0,1:T(8,128)} %param.8) | copy-start | bytes 393220
  3.0 0.9 %copy-start.2 = (s32[4096,8]{0,1:T(8,128)S(1)}, s32[4096,8]{0,1:T(8,128)}, u32[]{:S(2)}) copy-start(s32[4096,8]{0,1:T(8,128)} %param.9) | copy-start | bytes 393220
  3.9 0.9 %copy-start.3 = (f32[4096,8]{0,1:T(8,128)S(1)}, f32[4096,8]{0,1:T(8,128)}, u32[]{:S(2)}) copy-start(f32[4096,8]{0,1:T(8,128)} %param.10) | copy-start | bytes 393220
  4.8 0.8 %copy-start.4 = (bf16[2,128,128]{2,1,0:T(8,128)(2,1)S(1)}, bf16[2,128,128]{2,1,0:T(8,128)(2,1)}, u32[]{:S(2)}) copy-start(bf16[2,128,128]{2,1,0:T(8,128)(2,1)} %gate_ref.1) | copy-start | bytes 196612
  5.7 0.8 %copy-start.5 = (bf16[2,128,128]{2,1,0:T(8,128)(2,1)S(1)}, bf16[2,128,128]{2,1,0:T(8,128)(2,1)}, u32[]{:S(2)}) copy-start(bf16[2,128,128]{2,1,0:T(8,128)(2,1)} %up_ref.1) | copy-start | bytes 196612
  6.5 0.8 copy-start.6

commit v2 on v1

--- a/solution.py
+++ b/solution.py
@@ -31,26 +31,42 @@
     return lax.broadcasted_iota(jnp.int32, shape, dim)
 
 
+def quantize(t):
+    top = jnp.maximum(jnp.max(jnp.abs(t), axis=0, keepdims=True), 1e-30)
+    q = jnp.round(t * (32767.0 / top)).astype(jnp.int32).astype(jnp.int16)
+    return q, top * (1.0 / 32767.0)
+
+
 def turn(i):
     half = lax.div(i + 1, 2)
     return 4 + half * (1 - 2 * lax.rem(i, 2))
 
 
 def kernel(
-    ids_ref, slots_ref, comb_ref, g_ref, w_hbm, gate_ref, up_ref,
+    ids_hbm, slots_hbm, comb_hbm, g_hbm, w_hbm, gate_hbm, up_hbm,
     dg_ref, du_ref, dc_ref,
-    s1, r1, s2, r2, wv, xs, gm, gsel, a_gate, a_up, hid, qs, qr, cs, cr, acc,
-    ys, yr, ps, pr, zs, zr,
-    w_sem, s1_sem, r1_sem, s2_sem, r2_sem, qs_sem, qr_sem, cs_sem, cr_sem,
-    ys_sem, yr_sem, ps_sem, pr_sem, zs_sem, zr_sem,
+    ids_ref, slots_ref, comb_ref, g_ref, gate_ref, up_ref,
+    s1, r1, s2, r2, wv, xs, gm, gsel, a_gate, a_up, qs, qr, cs, cr, acc,
+    ys, yr, ps, pr, zs, zr, hs, hr, hcs, hcr, vv,
+    in_sem, s1_sem, r1_sem, s2_sem, r2_sem, qs_sem, qr_sem, cs_sem, cr_sem,
+    ys_sem, yr_sem, ps_sem, pr_sem, zs_sem, zr_sem, hs_sem, hr_sem, hcs_sem, hcr_sem,
 ):
     node = lax.axis_index("node")
     loc = lax.axis_index("local")
     zi = lax.div(node, NP)
     pi = lax.rem(node, NP)
 
-    w_copy = pltpu.make_async_copy(w_hbm, wv, w_sem)
-    w_copy.start()
+    loads = [
+        pltpu.make_async_copy(src, dst, in_sem.at[n])
+        for n, (src, dst) in enumerate(
+            (
+                (ids_hbm, ids_ref), (g_hbm, g_ref), (slots_hbm, slots_ref), (comb_hbm, comb_ref),
+                (gate_hbm, gate_ref), (up_hbm, up_ref), (w_hbm, wv),
+            )
+        )
+    ]
+    for load in loads:
+        load.start()
 
     def p_peer(d):
         return lax.rem(pi + d, NP)
@@ -75,6 +91,8 @@
     lax.fori_loop(1, NP, greet_p, 0)
     lax.fori_loop(1, NZ, greet_z, 0)
 
+    loads[0].wait()
+    loads[1].wait()
     base = pl.multiple_of(lax.div(node, 4) * 128, 128)
     ids_c = ids_ref[:, pl.ds(base, 128)]
     sub = lax.rem(node, 4)
@@ -91,6 +109,20 @@
     s1[:, :, 0:DL] = x.reshape(NP, NZ, DL)
     s1[:, :, DL:DPAD] = jnp.zeros((NP, NZ, DPAD - DL), BF16)
 
+    loads[4].wait()
+    loads[5].wait()
+    for e in range(2):
+        g = gate_ref[e].astype(F32)
+        u = up_ref[e].astype(F32)
+        sg = 1.0 / (1.0 + jnp.exp(-g))
+        gs = g * sg
+        a_up[e] = gs
+        a_gate[e] = u * sg * (1.0 + g * (1.0 - sg))
+        q, scale = quantize(gs * u)
+        hs[e] = q
+        hcs[e : e + 1, :] = scale
+    hr[pl.ds(loc, 1)] = hs[...].reshape(1, 2, CAP, HB)
+    hcr[pl.ds(loc, 1)] = hcs[...].reshape(1, 2, HB)
     pl.semaphore_wait(barrier, 2 * (NP - 1) + NZ - 1)
 
     def s1_copy(d, src, dst):
@@ -106,6 +138,28 @@
 
     lax.fori_loop(1, NP, s1_start, 0)
     r1[pl.ds(pi, 1)] = s1[pl.ds(pi, 1)]
+
+    def h_copy(d, dst):
+        return pltpu.make_async_remote_copy(
+            src_ref=hs, dst_ref=hr.at[dst],
+            send_sem=hs_sem.at[d], recv_sem=hr_sem.at[d],
+            device_id=(node, l_peer(d)), device_id_type=MESH,
+        )
+
+    def hc_copy(d, dst):
+        return pltpu.make_async_remote_copy(
+            src_ref=hcs, dst_ref=hcr.at[dst],
+            send_sem=hcs_sem.at[d], recv_sem=hcr_sem.at[d],
+            device_id=(node, l_peer(d)), device_id_type=MESH,
+        )
+
+    def h_start(i, c):
+        d = turn(i)
+        hc_copy(d, loc).start()
+        h_copy(d, loc).start()
+        return c
+
+    lax.fori_loop(0, NL - 1, h_start, 0)
 
     ri = iota((2 * NN, NN), 0)
     ci = iota((2 * NN, NN), 1)
@@ -137,6 +191,8 @@
     lax.fori_loop(1, NZ, s2_start, 0)
     r2[pl.ds(zi, 1)] = s2[pl.ds(zi, 1)]
 
+    loads[2].wait()
+    loads[3].wait()
     ids = ids_ref[...]
     slots = slots_ref[...].astype(F32)
     comb = comb_ref[...]
@@ -169,15 +225,42 @@
         sel_b = sel_f.astype(BF16)
         gsel[e, 0] = dot(sel_b, ex0).astype(BF16)
         gsel[e, 1] = dot(sel_b, ex1).astype(BF16)
-        g = gate_ref[e].astype(F32)
-        u = up_ref[e].astype(F32)
-        sg = 1.0 / (1.0 + jnp.exp(-g))
-        gs = g * sg
-        hid[e] = gs * u
-        a_up[e] = weight * gs
-        a_gate[e] = weight * (u * sg * (1.0 + g * (1.0 - sg)))
-
-    w_copy.wait()
+        a_up[e] = weight * a_up[e]
+        a_gate[e] = weight * a_gate[e]
+
+    loads[6].wait()
+
+    def h_wait(i, c):
+        d = turn(i)
+        l = lax.rem(loc + NL - d, NL)
+        hc_copy(d, l).wait_recv()
+        h_copy(d, l).wait_recv()
+        return c
+
+    lax.fori_loop(0, NL - 1, h_wait, 0)
+
+    vv[...] = jnp.zeros((2, CAP, DL), F32)
+
+    def back_project(j, c):
+        cols = pl.ds(pl.multiple_of(j * 2 * HB, 2 * HB), 2 * HB)
+        for e in range(2):
+            h = jnp.concatenate(
+                [
+                    hr[2 * j + b, e].astype(jnp.int32).astype(F32) * hcr[2 * j + b, e : e + 1, :]
+                    for b in range(2)
+                ],
+                axis=1,
+            )
+            top = h.astype(BF16)
+            rest = (h - top.astype(F32)).astype(BF16)
+            r = lax.dot_general(
+                jnp.concatenate([top, rest], axis=0), wv[e, :, cols],
+                (((1,), (1,)), ((), ())), preferred_element_type=F32,
+            )
+            vv[e] += r[:CAP] + r[CAP:]
+        return c
+
+    lax.fori_loop(0, NL // 2, back_project, 0)
 
     def s2_wait(d, c):
         s2_copy(d, z_peer(d), lax.rem(zi + NZ - d, NZ)).wait_recv()
@@ -188,6 +271,23 @@
     for e in range(2):
         xs[e, :, 0:256] = dot(gsel[e, 0], r2f).astype(BF16)
         xs[e, :, 256:512] = dot(gsel[e, 1], r2f).astype(BF16)
+    for e in range(2):
+        part = jnp.sum(xs[e, :, 0:DL].astype(F32) * vv[e], axis=1, keepdims=True)
+        ys[e : e + 1, :] = jnp.sum(gm[e] * part, axis=0, keepdims=True)
+
+    def y_copy(d, dst):
+        return pltpu.make_async_remote_copy(
+            src_ref=ys, dst_ref=yr.at[dst],
+            send_sem=ys_sem.at[d], recv_sem=yr_sem.at[d],
+            device_id=(node, l_peer(d)), device_id_type=MESH,
+        )
+
+    def y_start(i, c):
+        y_copy(turn(i), loc).start()
+        return c
+
+    lax.fori_loop(0, NL - 1, y_start, 0)
+    yr[pl.ds(loc, 1)] = ys[...].reshape(1, 2, NN)
 
     def q_copy(d, src, dst):
         return pltpu.make_async_remote_copy(
@@ -212,10 +312,9 @@
         l = l_peer(d)
         for e in range(2):
             t = project(e, l)
-            top = jnp.maximum(jnp.max(jnp.abs(t), axis=0, keepdims=True), 1e-30)
-            q = jnp.round(t * (32767.0 / top))
-            qs[l, e] = q.astype(jnp.int32).astype(jnp.int16)
-            cs[l, e : e + 1, :] = top * (1.0 / 32767.0)
+            q, scale = quantize(t)
+            qs[l, e] = q
+            cs[l, e : e + 1, :] = scale
         c_copy(d, l, loc).start()
         q_copy(d, l, loc).start()
         return c
@@ -223,40 +322,6 @@
     lax.fori_loop(0, NL - 1, send_block, 0)
     for e in range(2):
         acc[e] = project(e, loc)
-
-    def take_block(i, c):
-        d = turn(i)
-        l = lax.rem(loc + NL - d, NL)
-        c_copy(d, l_peer(d), l).wait_recv()
-        q_copy(d, l_peer(d), l).wait_recv()
-        for e in range(2):
-            acc[e] += qr[l, e].astype(jnp.int32).astype(F32) * cr[l, e : e + 1, :]
-        return c
-
-    lax.fori_loop(0, NL - 1, take_block, 0)
-
-    for e in range(2):
-        t = acc[e]
-        part = jnp.sum(hid[e] * t, axis=1, keepdims=True)
-        ys[e : e + 1, :] = jnp.sum(gm[e] * part, axis=0, keepdims=True)
-
-    def y_copy(d, dst):
-        return pltpu.make_async_remote_copy(
-            src_ref=ys, dst_ref=yr.at[dst],
-            send_sem=ys_sem.at[d], recv_sem=yr_sem.at[d],
-            device_id=(node, l_peer(d)), device_id_type=MESH,
-        )
-
-    def y_start(d, c):
-        y_copy(d, loc).start()
-        return c
-
-    lax.fori_loop(1, NL, y_start, 0)
-    yr[pl.ds(loc, 1)] = ys[...].reshape(1, 2, NN)
-    for e in range(2):
-        t = acc[e]
-        dg_ref[e] = (t * a_gate[e]).astype(BF16)
-        du_ref[e] = (t * a_up[e]).astype(BF16)
 
     def y_wait(d, c):
         y_copy(d, lax.rem(loc + NL - d, NL)).wait_recv()
@@ -307,6 +372,22 @@
     lax.fori_loop(1, NZ, z_start, 0)
     zr[pl.ds(zi, 1)] = packed.reshape(1, 2, NN)
 
+    def take_block(i, c):
+        d = turn(i)
+        l = lax.rem(loc + NL - d, NL)
+        c_copy(d, l_peer(d), l).wait_recv()
+        q_copy(d, l_peer(d), l).wait_recv()
+        for e in range(2):
+            acc[e] += qr[l, e].astype(jnp.int32).astype(F32) * cr[l, e : e + 1, :]
+        return c
+
+    lax.fori_loop(0, NL - 1, take_block, 0)
+
+    for e in range(2):
+        t = acc[e]
+        dg_ref[e] = (t * a_gate[e]).astype(BF16)
+        du_ref[e] = (t * a_up[e]).astype(BF16)
+
     choice = jnp.concatenate([ids_my[k : k + 1, :] for k in range(8)], axis=1)
     lane = (node + ((choice >> 1) & (NP - 1))) & (NN - 1)
     lane_hit = iota((NN, 256), 0) == lane
@@ -333,6 +414,8 @@
         q_copy(d, l_peer(d), loc).wait_send()
         c_copy(d, l_peer(d), loc).wait_send()
         y_copy(d, loc).wait_send()
+        h_copy(d, loc).wait_send()
+        hc_copy(d, loc).wait_send()
         p_copy(d, pi).wait_send()
         return c
 
@@ -355,9 +438,15 @@
             jax.ShapeDtypeStruct(gate_pre.shape, BF16),
             jax.ShapeDtypeStruct((8, 32), F32),
         ),
-        in_specs=[vmem, vmem, vmem, vmem, pl.BlockSpec(memory_space=pl.ANY), vmem, vmem],
+        in_specs=[pl.BlockSpec(memory_space=pltpu.HBM)] * 7,
         out_specs=(vmem, vmem, vmem),
         scratch_shapes=[
+            pltpu.VMEM((8, 4096), jnp.int32),
+            pltpu.VMEM((8, 4096), jnp.int32),
+            pltpu.VMEM((8, 4096), F32),
+            pltpu.VMEM((32, DL), BF16),
+            pltpu.VMEM((2, CAP, HB), BF16),
+            pltpu.VMEM((2, CAP, HB), BF16),
             pltpu.VMEM((NP, NZ, DPAD), BF16),
             pltpu.VMEM((NP, NZ, DPAD), BF16),
             pltpu.VMEM((NZ, 16, 256), BF16),
@@ -366,7 +455,6 @@
             pltpu.VMEM((2, CAP, DPAD), BF16),
             pltpu.VMEM((2, CAP, NN), F32),
             pltpu.VMEM((2, 2, CAP, 256), BF16),
-            pltpu.VMEM((2, CAP, HB), F32),
             pltpu.VMEM((2, CAP, HB), F32),
             pltpu.VMEM((2, CAP, HB), F32),
             pltpu.VMEM((NL, 2, CAP, HB), jnp.int16),
@@ -380,7 +468,12 @@
             pltpu.VMEM((NP, 2, NN), F32),
             pltpu.VMEM((2, NN), F32),
             pltpu.VMEM((NZ, 2, NN), F32),
-            dma,
+            pltpu.VMEM((2, CAP, HB), jnp.int16),
+            pltpu.VMEM((NL, 2, CAP, HB), jnp.int16),
+            pltpu.VMEM((2, HB), F32),
+            pltpu.VMEM((NL, 2, HB), F32),
+            pltpu.VMEM((2, CAP, DL), F32),
+            dma((7,)),
             dma((NP,)), dma((NP,)),
             dma((NZ,)), dma((NZ,)),
             dma((NL,)), dma((NL,)),
@@ -388,9 +481,11 @@
             dma((NL,)), dma((NL,)),
             dma((NP,)), dma((NP,)),
             dma((NZ,)), dma((NZ,)),
+            dma((NL,)), dma((NL,)),
+            dma((NL,)), dma((NL,)),
         ],
         compiler_params=pltpu.CompilerParams(
-            collective_id=0, has_side_effects=True, vmem_limit_bytes=32 * 1024 * 1024
+            collective_id=0, has_side_effects=True, vmem_limit_bytes=60 * 1024 * 1024
         ),
         name="routed_backward",
     )(

time: 78.6 us -> 63.1 us (0.80)
  Pallas kernels: 69 us -> 57.9 us
  local copies, waits for them, and re-layouts: 8.49 us -> 4.22 us
    pallas_call x1, Pallas kernels: 69 us -> 57.9 us  [shards(): pl.pallas_call(kernel, out_shape=(jax.ShapeDtypeStruct(gate_pre.shape, BF...]
    unnamed x17 -> x3, local copies, waits for them, and re-layouts: 8.49 us -> 4.22 us
where the time goes in v2:
time: 63.1 us; the launch traced here: 62.8 us
  Pallas kernels  57.9 us (92%)
  local copies, waits for them, and re-layouts  4.22 us (7%)
  between operations  0.64 us (1%)
    pallas_call x1, Pallas kernels, shards(): pl.pallas_call(kernel, out_shape=(jax.ShapeDtypeStruct(gate_pre.shape, BF...  57.9 us
    unnamed x3, local copies, waits for them, and re-layouts  4.22 us

profile of v2, /device:TPU:1, one launch (start us, length us, event | category | flops | bytes accessed | tf_op | source)
XLA Modules:
  0.0 62.8 jit_solution(14753140920239419506)
XLA Ops:
  0.6 57.9 %routed_backward.1 = (bf16[2,128,128]{2,1,0:T(8,128)(2,1)}, bf16[2,128,128]{2,1,0:T(8,128)(2,1)}, f32[8,32]{1,0:T(8,128)}) custom-call(s32[8,4096]{1,0:T(8,128)} %bitcast.6, s32[8,4096]{1,0:T(8,128)} %bitcast.7, f32[8,4096]{1,0:T(8,128)} %bitcast.8, bf16[32,448]{1,0:T(8,128)(2,1)} %g_hbm.1, bf16[2,448,1024]{2,1,0:T(8,128)(2,1)} %bitcast.5, ...), custom_call_target="tpu_custom_call" | custom-call | tf_op jit(solution)/shard_map/routed_backward/pallas_call | solution.py:434
  58.5 1.5 %copy.13 = bf16[2,128,128]{2,1,0:T(8,128)(2,1)} copy(bf16[2,128,128]{2,1,0:T(8,128)(2,1)} %get-tuple-element.12) | data formatting | bytes 131072
  60.0 1.5 %copy.14 = bf16[2,128,128]{2,1,0:T(8,128)(2,1)} copy(bf16[2,128,128]{2,1,0:T(8,128)(2,1)} %get-tuple-element.13) | data formatting | bytes 131072
  61.5 1.3 %copy.15 = f32[32,8]{0,1:T(8,128)} copy(f32[32,8]{0,1:T(8,128)} %bitcast.9) | data formatting | bytes 2048

commit v3 on v2

--- a/solution.py
+++ b/solution.py
@@ -42,31 +42,38 @@
     return 4 + half * (1 - 2 * lax.rem(i, 2))
 
 
+def z_turn(i):
+    half = lax.div(i + 1, 2)
+    return 8 + half * (1 - 2 * lax.rem(i, 2))
+
+
 def kernel(
     ids_hbm, slots_hbm, comb_hbm, g_hbm, w_hbm, gate_hbm, up_hbm,
     dg_ref, du_ref, dc_ref,
-    ids_ref, slots_ref, comb_ref, g_ref, gate_ref, up_ref,
+    near_ref, ids_ref, slots_ref, comb_ref, g_ref, gate_ref, up_ref,
     s1, r1, s2, r2, wv, xs, gm, gsel, a_gate, a_up, qs, qr, cs, cr, acc,
-    ys, yr, ps, pr, zs, zr, hs, hr, hcs, hcr, vv,
+    ys, yr, zs, zr, hs, hr, hcs, hcr, vv,
     in_sem, s1_sem, r1_sem, s2_sem, r2_sem, qs_sem, qr_sem, cs_sem, cr_sem,
-    ys_sem, yr_sem, ps_sem, pr_sem, zs_sem, zr_sem, hs_sem, hr_sem, hcs_sem, hcr_sem,
+    higher, ys_sem, yr_sem, zs_sem, zr_sem, hs_sem, hr_sem, hcs_sem, hcr_sem,
 ):
     node = lax.axis_index("node")
     loc = lax.axis_index("local")
     zi = lax.div(node, NP)
     pi = lax.rem(node, NP)
 
+    base = pl.multiple_of(lax.div(node, 4) * 128, 128)
     loads = [
         pltpu.make_async_copy(src, dst, in_sem.at[n])
         for n, (src, dst) in enumerate(
             (
-                (ids_hbm, ids_ref), (g_hbm, g_ref), (slots_hbm, slots_ref), (comb_hbm, comb_ref),
-                (gate_hbm, gate_ref), (up_hbm, up_ref), (w_hbm, wv),
+                (ids_hbm.at[:, pl.ds(base, 128)], near_ref), (g_hbm, g_ref),
+                (slots_hbm, slots_ref), (comb_hbm, comb_ref),
+                (gate_hbm, gate_ref), (up_hbm, up_ref), (w_hbm, wv), (ids_hbm, ids_ref),
             )
         )
     ]
-    for load in loads:
-        load.start()
+    for n in (0, 1, 4, 5, 7, 2, 3, 6):
+        loads[n].start()
 
     def p_peer(d):
         return lax.rem(pi + d, NP)
@@ -76,6 +83,15 @@
 
     def l_peer(d):
         return lax.rem(loc + d, NL)
+
+    late = jnp.where(jnp.logical_and(pi == 0, loc == 0), 1, 0)
+    rank = lax.rem(zi + late * (NZ - 1), NZ)
+
+    def plane(r):
+        return lax.rem(r + late, NZ)
+
+    def rank_of(z):
+        return lax.rem(z + late * (NZ - 1), NZ)
 
     barrier = pltpu.get_barrier_semaphore()
 
@@ -84,17 +100,22 @@
         pl.semaphore_signal(barrier, inc=1, device_id=(node, l_peer(d)), device_id_type=MESH)
         return c
 
-    def greet_z(d, c):
-        pl.semaphore_signal(barrier, inc=1, device_id=(z_peer(d) * NP + pi, loc), device_id_type=MESH)
+    def greet_z(k, c):
+        pl.semaphore_signal(barrier, inc=1, device_id=(plane(k) * NP + pi, loc), device_id_type=MESH)
+        return c
+
+    def answer_z(k, c):
+        pl.semaphore_signal(higher, inc=1, device_id=(plane(k) * NP + pi, loc), device_id_type=MESH)
         return c
 
     lax.fori_loop(1, NP, greet_p, 0)
-    lax.fori_loop(1, NZ, greet_z, 0)
+    lax.fori_loop(rank + 1, NZ, greet_z, 0)
+    pl.semaphore_wait(barrier, 2 * (NP - 1) + rank)
+    lax.fori_loop(0, rank, answer_z, 0)
 
     loads[0].wait()
     loads[1].wait()
-    base = pl.multiple_of(lax.div(node, 4) * 128, 128)
-    ids_c = ids_ref[:, pl.ds(base, 128)]
+    ids_c = near_ref[...]
     sub = lax.rem(node, 4)
     ids_my = ids_c[:, 0:32]
     for j in range(1, 4):
@@ -108,6 +129,21 @@
     x = dot(hit.astype(BF16), g_ref[...]).astype(BF16)
     s1[:, :, 0:DL] = x.reshape(NP, NZ, DL)
     s1[:, :, DL:DPAD] = jnp.zeros((NP, NZ, DPAD - DL), BF16)
+
+
+    def s1_copy(d, src, dst):
+        return pltpu.make_async_remote_copy(
+            src_ref=s1.at[src], dst_ref=r1.at[dst],
+            send_sem=s1_sem.at[d], recv_sem=r1_sem.at[d],
+            device_id=(zi * NP + p_peer(d), loc), device_id_type=MESH,
+        )
+
+    def s1_start(d, c):
+        s1_copy(d, p_peer(d), pi).start()
+        return c
+
+    lax.fori_loop(1, NP, s1_start, 0)
+    r1[pl.ds(pi, 1)] = s1[pl.ds(pi, 1)]
 
     loads[4].wait()
     loads[5].wait()
@@ -123,21 +159,6 @@
         hcs[e : e + 1, :] = scale
     hr[pl.ds(loc, 1)] = hs[...].reshape(1, 2, CAP, HB)
     hcr[pl.ds(loc, 1)] = hcs[...].reshape(1, 2, HB)
-    pl.semaphore_wait(barrier, 2 * (NP - 1) + NZ - 1)
-
-    def s1_copy(d, src, dst):
-        return pltpu.make_async_remote_copy(
-            src_ref=s1.at[src], dst_ref=r1.at[dst],
-            send_sem=s1_sem.at[d], recv_sem=r1_sem.at[d],
-            device_id=(zi * NP + p_peer(d), loc), device_id_type=MESH,
-        )
-
-    def s1_start(d, c):
-        s1_copy(d, p_peer(d), pi).start()
-        return c
-
-    lax.fori_loop(1, NP, s1_start, 0)
-    r1[pl.ds(pi, 1)] = s1[pl.ds(pi, 1)]
 
     def h_copy(d, dst):
         return pltpu.make_async_remote_copy(
@@ -184,13 +205,25 @@
             device_id=(z_peer(d) * NP + pi, loc), device_id_type=MESH,
         )
 
-    def s2_start(d, c):
+    def s2_start(d):
         s2_copy(d, z_peer(d), zi).start()
-        return c
-
-    lax.fori_loop(1, NZ, s2_start, 0)
+
+    def s2_lower(i, c):
+        d = z_turn(i)
+        pl.when(rank_of(z_peer(d)) < rank)(lambda: s2_start(d))
+        return c
+
+    def s2_higher(i, c):
+        d = z_turn(i)
+        pl.when(rank_of(z_peer(d)) > rank)(lambda: s2_start(d))
+        return c
+
+    lax.fori_loop(0, NZ - 1, s2_lower, 0)
+    pl.when(rank < NZ - 1)(lambda: pl.semaphore_wait(higher, NZ - 1 - rank))
+    lax.fori_loop(0, NZ - 1, s2_higher, 0)
     r2[pl.ds(zi, 1)] = s2[pl.ds(zi, 1)]
 
+    loads[7].wait()
     loads[2].wait()
     loads[3].wait()
     ids = ids_ref[...]
@@ -230,37 +263,32 @@
 
     loads[6].wait()
 
-    def h_wait(i, c):
-        d = turn(i)
-        l = lax.rem(loc + NL - d, NL)
-        hc_copy(d, l).wait_recv()
-        h_copy(d, l).wait_recv()
-        return c
-
-    lax.fori_loop(0, NL - 1, h_wait, 0)
-
-    vv[...] = jnp.zeros((2, CAP, DL), F32)
-
-    def back_project(j, c):
-        cols = pl.ds(pl.multiple_of(j * 2 * HB, 2 * HB), 2 * HB)
+    def back_project(l, first):
+        cols = pl.ds(pl.multiple_of(l * HB, HB), HB)
         for e in range(2):
-            h = jnp.concatenate(
-                [
-                    hr[2 * j + b, e].astype(jnp.int32).astype(F32) * hcr[2 * j + b, e : e + 1, :]
-                    for b in range(2)
-                ],
-                axis=1,
-            )
+            h = hr[l, e].astype(jnp.int32).astype(F32) * hcr[l, e : e + 1, :]
             top = h.astype(BF16)
             rest = (h - top.astype(F32)).astype(BF16)
             r = lax.dot_general(
                 jnp.concatenate([top, rest], axis=0), wv[e, :, cols],
                 (((1,), (1,)), ((), ())), preferred_element_type=F32,
             )
-            vv[e] += r[:CAP] + r[CAP:]
-        return c
-
-    lax.fori_loop(0, NL // 2, back_project, 0)
+            r = r[:CAP] + r[CAP:]
+            if first:
+                vv[e] = r
+            else:
+                vv[e] += r
+
+    def h_take(i, c):
+        d = turn(i)
+        l = lax.rem(loc + NL - d, NL)
+        hc_copy(d, l).wait_recv()
+        h_copy(d, l).wait_recv()
+        back_project(l, False)
+        return c
+
+    back_project(loc, True)
+    lax.fori_loop(0, NL - 1, h_take, 0)
 
     def s2_wait(d, c):
         s2_copy(d, z_peer(d), lax.rem(zi + NZ - d, NZ)).wait_recv()
@@ -275,19 +303,20 @@
         part = jnp.sum(xs[e, :, 0:DL].astype(F32) * vv[e], axis=1, keepdims=True)
         ys[e : e + 1, :] = jnp.sum(gm[e] * part, axis=0, keepdims=True)
 
-    def y_copy(d, dst):
-        return pltpu.make_async_remote_copy(
-            src_ref=ys, dst_ref=yr.at[dst],
-            send_sem=ys_sem.at[d], recv_sem=yr_sem.at[d],
-            device_id=(node, l_peer(d)), device_id_type=MESH,
+    def y_copy(i):
+        dp, dl = lax.div(i, NL), lax.rem(i, NL)
+        return pltpu.make_async_remote_copy(
+            src_ref=ys, dst_ref=yr.at[i],
+            send_sem=ys_sem.at[i], recv_sem=yr_sem.at[i],
+            device_id=(zi * NP + p_peer(dp), l_peer(dl)), device_id_type=MESH,
         )
 
     def y_start(i, c):
-        y_copy(turn(i), loc).start()
-        return c
-
-    lax.fori_loop(0, NL - 1, y_start, 0)
-    yr[pl.ds(loc, 1)] = ys[...].reshape(1, 2, NN)
+        y_copy(i).start()
+        return c
+
+    lax.fori_loop(1, NP * NL, y_start, 0)
+    yr[0] = ys[...]
 
     def q_copy(d, src, dst):
         return pltpu.make_async_remote_copy(
@@ -323,36 +352,15 @@
     for e in range(2):
         acc[e] = project(e, loc)
 
-    def y_wait(d, c):
-        y_copy(d, lax.rem(loc + NL - d, NL)).wait_recv()
-        return c
-
-    lax.fori_loop(1, NL, y_wait, 0)
-    ps[...] = jnp.sum(yr[...], axis=0)
-
-    def p_copy(d, dst):
-        return pltpu.make_async_remote_copy(
-            src_ref=ps, dst_ref=pr.at[dst],
-            send_sem=ps_sem.at[d], recv_sem=pr_sem.at[d],
-            device_id=(zi * NP + p_peer(d), loc), device_id_type=MESH,
-        )
-
-    def p_start(d, c):
-        p_copy(d, pi).start()
-        return c
-
-    lax.fori_loop(1, NP, p_start, 0)
-    pr[pl.ds(pi, 1)] = ps[...].reshape(1, 2, NN)
-
-    def p_wait(d, c):
-        p_copy(d, lax.rem(pi + NP - d, NP)).wait_recv()
-        return c
-
-    lax.fori_loop(1, NP, p_wait, 0)
+    def y_wait(i, c):
+        y_copy(i).wait_recv()
+        return c
+
+    lax.fori_loop(1, NP * NL, y_wait, 0)
     to_here = (iota((2, NN), 1) & (NP - 1)) == pi
     packed = jnp.zeros((2, NN), F32)
     for q in range(NP):
-        v = jnp.where(to_here, pr[q], 0.0)
+        v = jnp.where(to_here, jnp.sum(yr[q * NL : (q + 1) * NL], axis=0), 0.0)
         if q:
             v = jnp.concatenate([v[:, NN - q :], v[:, : NN - q]], axis=1)
         packed = packed + v
@@ -365,11 +373,11 @@
             device_id=(z_peer(d) * NP + pi, loc), device_id_type=MESH,
         )
 
-    def z_start(d, c):
-        z_copy(d, zi).start()
-        return c
-
-    lax.fori_loop(1, NZ, z_start, 0)
+    def z_start(i, c):
+        z_copy(z_turn(i), zi).start()
+        return c
+
+    lax.fori_loop(0, NZ - 1, z_start, 0)
     zr[pl.ds(zi, 1)] = packed.reshape(1, 2, NN)
 
     def take_block(i, c):
@@ -389,7 +397,7 @@
         du_ref[e] = (t * a_up[e]).astype(BF16)
 
     choice = jnp.concatenate([ids_my[k : k + 1, :] for k in range(8)], axis=1)
-    lane = (node + ((choice >> 1) & (NP - 1))) & (NN - 1)
+    lane = (node + ((pi - (choice >> 1)) & (NP - 1))) & (NN - 1)
     lane_hit = iota((NN, 256), 0) == lane
     plane_hit = iota((NZ, 256), 0) == (choice >> 4)
     member = choice & 1
@@ -413,10 +421,8 @@
         s1_copy(d, p_peer(d), pi).wait_send()
         q_copy(d, l_peer(d), loc).wait_send()
         c_copy(d, l_peer(d), loc).wait_send()
-        y_copy(d, loc).wait_send()
         h_copy(d, loc).wait_send()
         hc_copy(d, loc).wait_send()
-        p_copy(d, pi).wait_send()
         return c
 
     def drain16(d, c):
@@ -424,7 +430,12 @@
         z_copy(d, zi).wait_send()
         return c
 
+    def drain64(i, c):
+        y_copy(i).wait_send()
+        return c
+
     lax.fori_loop(1, NP, drain8, 0)
+    lax.fori_loop(1, NP * NL, drain64, 0)
     lax.fori_loop(1, NZ, drain16, 0)
 
 
@@ -441,6 +452,7 @@
         in_specs=[pl.BlockSpec(memory_space=pltpu.HBM)] * 7,
         out_specs=(vmem, vmem, vmem),
         scratch_shapes=[
+            pltpu.VMEM((8, 128), jnp.int32),
             pltpu.VMEM((8, 4096), jnp.int32),
             pltpu.VMEM((8, 4096), jnp.int32),
             pltpu.VMEM((8, 4096), F32),
@@ -463,9 +475,7 @@
             pltpu.VMEM((NL, 2, HB), F32),
             pltpu.VMEM((2, CAP, HB), F32),
             pltpu.VMEM((2, NN), F32),
-            pltpu.VMEM((NL, 2, NN), F32),
-            pltpu.VMEM((2, NN), F32),
-            pltpu.VMEM((NP, 2, NN), F32),
+            pltpu.VMEM((NP * NL, 2, NN), F32),
             pltpu.VMEM((2, NN), F32),
             pltpu.VMEM((NZ, 2, NN), F32),
             pltpu.VMEM((2, CAP, HB), jnp.int16),
@@ -473,13 +483,13 @@
             pltpu.VMEM((2, HB), F32),
             pltpu.VMEM((NL, 2, HB), F32),
             pltpu.VMEM((2, CAP, DL), F32),
-            dma((7,)),
+            dma((8,)),
             dma((NP,)), dma((NP,)),
             dma((NZ,)), dma((NZ,)),
             dma((NL,)), dma((NL,)),
             dma((NL,)), dma((NL,)),
-            dma((NL,)), dma((NL,)),
-            dma((NP,)), dma((NP,)),
+            pltpu.SemaphoreType.REGULAR,
+            dma((NP * NL,)), dma((NP * NL,)),
             dma((NZ,)), dma((NZ,)),
             dma((NL,)), dma((NL,)),
             dma((NL,)), dma((NL,)),

time: 63.1 us -> 61.2 us (0.970)
  Pallas kernels: 57.9 us -> 56.1 us
    pallas_call x1, Pallas kernels: 57.9 us -> 56.1 us  [shards(): pl.pallas_call(kernel, out_shape=(jax.ShapeDtypeStruct(gate_pre.shape, BF...]
where the time goes in v3:
time: 61.2 us; the launch traced here: 61 us
  Pallas kernels  56.1 us (92%)
  local copies, waits for them, and re-layouts  4.22 us (7%)
  between operations  0.64 us (1%)
    pallas_call x1, Pallas kernels, shards(): pl.pallas_call(kernel, out_shape=(jax.ShapeDtypeStruct(gate_pre.shape, BF...  56.1 us
    unnamed x3, local copies, waits for them, and re-layouts  4.22 us

profile of v3, /device:TPU:1, one launch (start us, length us, event | category | flops | bytes accessed | tf_op | source)
XLA Modules:
  0.0 61.0 jit_solution(5350682847462008081)
XLA Ops:
  0.6 56.1 %routed_backward.1 = (bf16[2,128,128]{2,1,0:T(8,128)(2,1)}, bf16[2,128,128]{2,1,0:T(8,128)(2,1)}, f32[8,32]{1,0:T(8,128)}) custom-call(s32[8,4096]{1,0:T(8,128)} %bitcast.6, s32[8,4096]{1,0:T(8,128)} %bitcast.7, f32[8,4096]{1,0:T(8,128)} %bitcast.8, bf16[32,448]{1,0:T(8,128)(2,1)} %g_hbm.1, bf16[2,448,1024]{2,1,0:T(8,128)(2,1)} %bitcast.5, ...), custom_call_target="tpu_custom_call" | custom-call | tf_op jit(solution)/shard_map/routed_backward/pallas_call | solution.py:445
  56.8 1.5 %copy.13 = bf16[2,128,128]{2,1,0:T(8,128)(2,1)} copy(bf16[2,128,128]{2,1,0:T(8,128)(2,1)} %get-tuple-element.12) | data formatting | bytes 131072
  58.2 1.5 %copy.14 = bf16[2,128,128]{2,1,0:T(8,128)(2,1)} copy(bf16[2,128,128]{2,1,0:T(8,128)(2,1)} %get-tuple-element.13) | data formatting | bytes 131072
  59.7 1.3 %copy.15 = f32[32,8]{0,1:T(8,128)} copy(f32[32,8]{0,1:T(8,128)} %bitcast.9) | data formatting | bytes 2048
